TPU v7x, 1024 devices: a whole 4x4x32 slice. The times are simulated.
1024 devices in a mesh: ctx: 64 (over z, x_hi), head: 8 (over y, x_lo), fsdp: 2 (over core).
Axes of the slice: x: 4 (x_hi: 2, x_lo: 2; x = x_hi * 2 + x_lo), y: 4, z: 32, core: 2. Of those that a mesh axis runs over, the one named last changes fastest.
Arguments:
- query_rows: bfloat16 [65536, 6144], P(('ctx', 'head'), 'fsdp'), may hold values from -400 to 400
- key_rows: bfloat16 [65536, 6144], P(('ctx', 'head'), 'fsdp'), may hold values from -8 to 8
- value_rows: bfloat16 [65536, 4096], P(('ctx', 'head'), 'fsdp'), may hold values from -6 to 6
- query_weight: bfloat16 [1536, 6144], P(('ctx', 'fsdp'), 'head'), may hold values from -6 to 6
- key_weight: bfloat16 [512, 4096], P(('ctx', 'fsdp'), 'head'), may hold values from -6 to 6
Outputs:
- attended: bfloat16 [65536, 4096], P('ctx', ('fsdp', 'head'))
- clipped_query: bfloat16 [1536, 6144], P(('ctx', 'fsdp'), 'head')
- clipped_key: bfloat16 [512, 4096], P(('ctx', 'fsdp'), 'head')
All inputs are finite; a program needn't handle non-finite values.
Results may differ from a plain program's by a relative error of at most 0.0033.
Values may be sent and summed in bfloat16 or wider, within the bound.
A program may use at most 64 MiB of HBM per device.

v0:
```python
import jax
import jax.numpy as jnp
from jax import lax
from jax.sharding import PartitionSpec as P

DNOPE = 128
DROPE = 64
DV = 128
DQK = 192


clip_threshold = 100.0


def shifted_2(value, axis, steps):
    count = lax.axis_size(axis)
    first, last = (max(0, -steps), min(count, count - steps))
    return lax.ppermute(value, axis, [(source, source + steps) for source in range(first, last)])


def from_everyone(shard, axis):
    copies = jnp.broadcast_to(shard, (lax.axis_size(axis), *shard.shape))
    return lax.all_to_all(copies, axis, split_axis=0, concat_axis=0, tiled=True)


def over_copies(shard, axis):
    everything = from_everyone(shard, axis)
    return jnp.max(everything, axis=0)


def laid_out(parts, dim):
    parts = jnp.moveaxis(parts, 0, dim)
    dims = parts.shape
    return parts.reshape(*dims[:dim], dims[dim] * dims[dim + 1], *dims[dim + 2 :])


def gathered_copies(shard, axis, dim):
    parts = from_everyone(shard, axis)
    return laid_out(parts, dim)


def partial_softmax(scores, value_cube):
    highest = jnp.max(scores, axis=2)
    present = jnp.isfinite(highest)
    shifted = jnp.where(present, highest, 0.0)
    weights = jnp.exp(scores - shifted[:, :, None])
    totals = jnp.sum(weights, axis=2)
    rounded = weights.astype(jnp.bfloat16)
    summed = jnp.einsum("htu,uhd->thd", rounded, value_cube, preferred_element_type=jnp.float32)
    return (summed, totals, jnp.where(present, highest, -jnp.inf))


def merge_parts(own_part, far_part):
    own_sum, own_total, own_high = own_part
    far_sum, far_total, far_high = far_part
    highest = jnp.maximum(own_high, far_high)
    own_scale = jnp.exp(own_high - highest)
    far_scale = jnp.exp(far_high - highest)
    totals = own_total * own_scale + far_total * far_scale
    mixed = own_sum * own_scale.T[:, :, None] + far_sum * far_scale.T[:, :, None]
    return mixed / totals.T[:, :, None]


def head_scores(query_cube, key_cube):
    return jnp.einsum(
        "thd,uhd->htu", query_cube, key_cube, preferred_element_type=jnp.float32
    ) * DQK ** (-0.5)


def causal_block(query_cube, key_cube, value_cube, row_start, block_rows):
    row_count = key_cube.shape[0]
    query_block = query_cube[row_start : row_start + block_rows]
    row_ids = lax.broadcasted_iota(jnp.int32, (block_rows, row_count), 0) + row_start
    col_ids = lax.broadcasted_iota(jnp.int32, (block_rows, row_count), 1)
    scores = jnp.where((row_ids >= col_ids)[None], head_scores(query_block, key_cube), -jnp.inf)
    return (partial_softmax(scores, value_cube), jnp.max(scores, axis=(1, 2)))


def body(query_rows, key_rows, value_rows, query_weight, key_weight):
    local_query, local_key, local_value = (
        lax.all_to_all(query_rows, "head", split_axis=1, concat_axis=0, tiled=True),
        lax.all_to_all(key_rows, "head", split_axis=1, concat_axis=0, tiled=True),
        lax.all_to_all(value_rows, "head", split_axis=1, concat_axis=0, tiled=True),
    )
    row_count = local_query.shape[0]
    head_count = local_query.shape[1] // DQK
    query_cube = local_query.reshape(row_count, head_count, DQK)
    key_cube = local_key.reshape(row_count, head_count, DQK)
    value_cube = local_value.reshape(row_count, head_count, DV)
    block_index = lax.axis_index("ctx")
    block_rows = min(512, row_count)
    row_starts = list(range(0, row_count, block_rows))
    local_peak = jnp.full((head_count,), -jnp.inf, jnp.float32)
    pieces = []
    far_key, far_value = shifted_2((local_key, local_value), "ctx", 1)
    far_keys = far_key.reshape(row_count, head_count, DQK)
    far_values = far_value.reshape(row_count, head_count, DV)
    for row_start in row_starts:
        own_part, own_peak = causal_block(query_cube, key_cube, value_cube, row_start, block_rows)
        far_scores = jnp.where(
            block_index > 0,
            head_scores(query_cube[row_start : row_start + block_rows], far_keys),
            -jnp.inf,
        )
        far_part = partial_softmax(far_scores, far_values)
        local_peak = jnp.maximum(
            local_peak, jnp.maximum(own_peak, jnp.max(far_scores, axis=(1, 2)))
        )
        pieces.append(merge_parts(own_part, far_part))
    attended = (
        jnp.concatenate(pieces, axis=0).astype(jnp.bfloat16).reshape(row_count, head_count * DV)
    )
    weight_heads = key_weight.shape[1] // DNOPE
    cycle_peak = over_copies(local_peak, "ctx")
    gathered = gathered_copies(cycle_peak, ("head", "fsdp"), 0)
    head_peak = (
        gathered.reshape(lax.axis_size("head"), lax.axis_size("fsdp"), head_count)
        .transpose(1, 0, 2)
        .reshape(-1)
    )
    own_peaks = lax.dynamic_slice_in_dim(
        head_peak, lax.axis_index("head") * weight_heads, weight_heads, 0
    )
    factor = jnp.minimum(1.0, clip_threshold / own_peaks)
    root_factor = jnp.sqrt(factor)
    column_factor = jnp.concatenate(
        [
            jnp.broadcast_to(root_factor[:, None], (weight_heads, DNOPE)),
            jnp.broadcast_to(factor[:, None], (weight_heads, DROPE)),
        ],
        axis=1,
    )
    query_count = query_weight.shape[0]
    key_count = key_weight.shape[0]
    clipped_query = (
        (
            query_weight.astype(jnp.float32).reshape(query_count, weight_heads, DQK)
            * column_factor[None]
        )
        .astype(jnp.bfloat16)
        .reshape(query_count, weight_heads * DQK)
    )
    clipped_key = (
        (
            key_weight.astype(jnp.float32).reshape(key_count, weight_heads, DNOPE)
            * root_factor[None, :, None]
        )
        .astype(jnp.bfloat16)
        .reshape(key_count, weight_heads * DNOPE)
    )
    return (attended, clipped_query, clipped_key)


def solution(mesh):
    return jax.shard_map(
        body,
        mesh=mesh,
        in_specs=(
            P(("ctx", "head"), "fsdp"),
            P(("ctx", "head"), "fsdp"),
            P(("ctx", "head"), "fsdp"),
            P(("ctx", "fsdp"), "head"),
            P(("ctx", "fsdp"), "head"),
        ),
        out_specs=(
            P("ctx", ("fsdp", "head")),
            P(("ctx", "fsdp"), "head"),
            P(("ctx", "fsdp"), "head"),
        ),
        check_vma=False,
    )
```

profile of v0, /device:TPU:1, one launch (start us, length us, event | category | flops | bytes accessed | tf_op | source)
XLA Modules:
  0.0 157.7 jit_solution(4806783634513867229)
XLA Ops:
  0.6 2.1 %copy.66 = bf16[128,2048]{0,1:T(8,128)(2,1)} copy(bf16[128,2048]{1,0:T(8,128)(2,1)} %param.7) | data formatting | bytes 1048576 | tf_op args[2]
  2.8 5.9 %all-to-all-start.2 = ((bf16[128,8,256]{0,2,1:T(8,128)(2,1)}), bf16[128,8,256]{0,2,1:T(8,128)(2,1)S(1)}, u32[]{:S(2)}, u32[]{:S(2)}) async-start(bf16[128,8,256]{0,2,1:T(8,128)(2,1)} %bitcast.5), calls=%async_computation.2 | async-start | bytes 1048576 | tf_op jit(solution)/shard_map/all_to_all | solution.py:83
  8.7 2.3 %copy.63 = bf16[128,3072]{0,1:T(8,128)(2,1)} copy(bf16[128,3072]{1,0:T(8,128)(2,1)} %param.6) | data formatting | bytes 1572864 | tf_op args[1]
  11.0 5.2 %all-to-all-done.2 = bf16[128,8,256]{0,2,1:T(8,128)(2,1)S(1)} async-done(((bf16[128,8,256]{0,2,1:T(8,128)(2,1)}), bf16[128,8,256]{0,2,1:T(8,128)(2,1)S(1)}, u32[]{:S(2)}, u32[]{:S(2)}) %all-to-all-start.2) | async-done | bytes 524320 | tf_op jit(solution)/shard_map/all_to_all | solution.py:83
  16.2 3.5 %all-to-all-start.1 = ((bf16[128,8,384]{0,2,1:T(8,128)(2,1)}), bf16[128,8,384]{0,2,1:T(8,128)(2,1)S(1)}, u32[]{:S(2)}, u32[]{:S(2)}) async-start(bf16[128,8,384]{0,2,1:T(8,128)(2,1)} %bitcast.2), calls=%async_computation.1 | async-start | bytes 1572864 | tf_op jit(solution)/shard_map/all_to_all | solution.py:82
  21.0 10.5 %all-to-all-done.1 = bf16[128,8,384]{0,2,1:T(8,128)(2,1)S(1)} async-done(((bf16[128,8,384]{0,2,1:T(8,128)(2,1)}), bf16[128,8,384]{0,2,1:T(8,128)(2,1)S(1)}, u32[]{:S(2)}, u32[]{:S(2)}) %all-to-all-start.1) | async-done | bytes 786464 | tf_op jit(solution)/shard_map/all_to_all | solution.py:82
  31.5 3.5 %all-to-all-start = ((bf16[128,8,384]{0,2,1:T(8,128)(2,1)}), bf16[128,8,384]{0,2,1:T(8,128)(2,1)S(1)}, u32[]{:S(2)}, u32[]{:S(2)}) async-start(bf16[128,8,384]{0,2,1:T(8,128)(2,1)} %bitcast), calls=%async_computation | async-start | bytes 1572864 | tf_op jit(solution)/shard_map/all_to_all | solution.py:81
  36.7 2.1 %reshape.106 = bf16[1024,2,128]{0,2,1:T(8,128)(2,1)} reshape(bf16[8,128,256]{1,0,2:T(8,128)(2,1)} %copy.68) | data formatting | bytes 1048576 | tf_op jit(solution)/shard_map/reshape | solution.py:89
  39.8 6.2 %collective-permute-start.1 = (bf16[1024,256]{1,0:T(8,128)(2,1)}, bf16[1024,256]{1,0:T(8,128)(2,1)}, u32[]{:S(2)}, u32[]{:S(2)}) collective-permute-start(bf16[1024,256]{1,0:T(8,128)(2,1)} %bitcast.127), channel_id=1, source_target_pairs={{0,16},{16,32},{32,48},{48,64},{64,80},{80,96},{96,112},{112,128},... | collective-permute-start | bytes 1572872 | tf_op jit(solution)/shard_map/ppermute | solution.py:18
  45.9 1.2 copy.64
  47.2 3.9 %collective-permute-start = (bf16[1024,384]{1,0:T(8,128)(2,1)}, bf16[1024,384]{1,0:T(8,128)(2,1)}, u32[]{:S(2)}, u32[]{:S(2)}) collective-permute-start(bf16[1024,384]{1,0:T(8,128)(2,1)} %bitcast.122), channel_id=1, source_target_pairs={{0,16},{16,32},{32,48},{48,64},{64,80},{80,96},{96,112},{112,128},... | collective-permute-start | bytes 2359304 | tf_op jit(solution)/shard_map/ppermute | solution.py:18
  52.9 1.2 fusion.13
  54.1 1.2 fusion.9
  55.3 3.0 %fusion.8 = (f32[2]{0:T(128)S(1)}, f32[2,512]{1,0:T(2,128)S(1)}, f32[2,512]{1,0:T(2,128)S(1)}, f32[2]{0:T(128)S(1)}) fusion(f32[2,512,1024]{2,1,0:T(8,128)S(1)} %get-tuple-element.26, pred[512,1024]{1,0:T(8,128)(4,1)S(1)} %iota_compare_fusion.1, f32[2,512]{1,0:T(2,128)S(1)} %is-finite_select_fusion.7, f32[2,512]{1,0:T(2,128)S(1)} %is-finite_select_fusion.3, ...), kind=kLoop, calls=%fused_computation.16 | loop fusion | flops 10483708 | bytes 9453584 | tf_op jit(solution)/shard_map/reduce_max | solution.py:76
  58.3 1.2 copy.70
  59.5 7.1 %collective-permute-done = bf16[1024,384]{1,0:T(8,128)(2,1)} collective-permute-done((bf16[1024,384]{1,0:T(8,128)(2,1)}, bf16[1024,384]{1,0:T(8,128)(2,1)}, u32[]{:S(2)}, u32[]{:S(2)}) %collective-permute-start) | collective-permute-done | bytes 786464 | tf_op jit(solution)/shard_map/ppermute | solution.py:18
  66.6 1.4 copy.69
  69.8 2.3 %fusion.10 = (f32[2]{0:T(128)S(1)}, f32[2,512]{1,0:T(2,128)S(1)}, f32[2,512]{1,0:T(2,128)S(1)}, f32[2]{0:T(128)S(1)}) fusion(f32[2,512,1024]{2,1,0:T(8,128)S(1)} %get-tuple-element.28, pred[]{:T(512)S(6)} %gt.4, f32[2,512]{1,0:T(2,128)S(1)} %is-finite_select_fusion.4, f32[2,512]{1,0:T(2,128)S(1)} %is-finite_select_fusion, ...), kind=kLoop, calls=%fused_computation.18 | loop fusion | flops 10483708 | bytes 8405009 | tf_op jit(solution)/shard_map/reduce_max | solution.py:107
  72.7 36.9 %all-to-all-start.3 = ((f32[64,1,2]{2,1,0:T(1,128)}), f32[64,1,2]{2,1,0:T(1,128)S(1)}, u32[]{:S(2)}, u32[]{:S(2)}) async-start(f32[64,1,2]{2,1,0:T(1,128)} %broadcast_in_dim.71), calls=%async_computation.3 | async-start | bytes 65536 | tf_op jit(solution)/shard_map/all_to_all | solution.py:23
  109.7 3.6 %fusion.55 = f32[512,2,128]{0,2,1:T(8,128)S(1)} fusion(bf16[1024,2,128]{0,2,1:T(8,128)(2,1)S(1)} %copy-done.8, f32[2,512,1024]{2,1,0:T(8,128)} %copy-done.2, f32[2,512]{1,0:T(2,128)S(1)} %is-finite_select_fusion.7, pred[512,1024]{1,0:T(8,128)(4,1)S(1)} %iota_compare_fusion.1, f32[512,2]{0,1:T(2,128)S(1)} %get-tuple-element.15), kind=kOutput, calls=%fused_computation.43 | convolution fusion | flops 272760832 | bytes 5775360 | tf_op jit(solution)/shard_map/htu,uhd->thd/dot_general | solution.py:49
  113.4 1.3 fusion.52
  119.1 13.8 %all-to-all-done.3 = f32[64,1,2]{2,1,0:T(1,128)S(1)} async-done(((f32[64,1,2]{2,1,0:T(1,128)}), f32[64,1,2]{2,1,0:T(1,128)S(1)}, u32[]{:S(2)}, u32[]{:S(2)}) %all-to-all-start.3) | async-done | bytes 544 | tf_op jit(solution)/shard_map/all_to_all | solution.py:23
  133.6 17.0 %all-to-all-start.4 = ((f32[16,1,2]{2,1,0:T(1,128)}), f32[16,1,2]{2,1,0:T(1,128)S(1)}, u32[]{:S(2)}, u32[]{:S(2)}) async-start(f32[16,1,2]{2,1,0:T(1,128)} %broadcast_in_dim.72), calls=%async_computation.4 | async-start | bytes 16384 | tf_op jit(solution)/shard_map/all_to_all | solution.py:23
  151.5 4.6 %all-to-all-done.4 = f32[16,1,2]{2,1,0:T(1,128)S(1)} async-done(((f32[16,1,2]{2,1,0:T(1,128)}), f32[16,1,2]{2,1,0:T(1,128)S(1)}, u32[]{:S(2)}, u32[]{:S(2)}) %all-to-all-start.4) | async-done | bytes 160 | tf_op jit(solution)/shard_map/all_to_all | solution.py:23
  (64 shorter events, 15.7 us)
Async XLA Ops:
  0.6 19.2 %copy-start.7 = (bf16[128,3072]{1,0:T(8,128)(2,1)S(1)}, bf16[128,3072]{1,0:T(8,128)(2,1)}, u32[]{:S(2)}) copy-start(bf16[128,3072]{1,0:T(8,128)(2,1)} %param.5) | copy-start | bytes 2359300
  2.8 13.5 %all-to-all-start.2 = ((bf16[128,8,256]{0,2,1:T(8,128)(2,1)}), bf16[128,8,256]{0,2,1:T(8,128)(2,1)S(1)}, u32[]{:S(2)}, u32[]{:S(2)}) async-start(bf16[128,8,256]{0,2,1:T(8,128)(2,1)} %bitcast.5), calls=%async_computation.2 | async-start | bytes 1048576 | tf_op jit(solution)/shard_map/all_to_all | solution.py:83
  16.2 15.2 %all-to-all-start.1 = ((bf16[128,8,384]{0,2,1:T(8,128)(2,1)}), bf16[128,8,384]{0,2,1:T(8,128)(2,1)S(1)}, u32[]{:S(2)}, u32[]{:S(2)}) async-start(bf16[128,8,384]{0,2,1:T(8,128)(2,1)} %bitcast.2), calls=%async_computation.1 | async-start | bytes 1572864 | tf_op jit(solution)/shard_map/all_to_all | solution.py:82
  31.5 19.6 %all-to-all-start = ((bf16[128,8,384]{0,2,1:T(8,128)(2,1)}), bf16[128,8,384]{0,2,1:T(8,128)(2,1)S(1)}, u32[]{:S(2)}, u32[]{:S(2)}) async-start(bf16[128,8,384]{0,2,1:T(8,128)(2,1)} %bitcast), calls=%async_computation | async-start | bytes 1572864 | tf_op jit(solution)/shard_map/all_to_all | solution.py:81
  39.8 18.5 %collective-permute-start.1 = (bf16[1024,256]{1,0:T(8,128)(2,1)}, bf16[1024,256]{1,0:T(8,128)(2,1)}, u32[]{:S(2)}, u32[]{:S(2)}) collective-permute-start(bf16[1024,256]{1,0:T(8,128)(2,1)} %bitcast.127), channel_id=1, source_target_pairs={{0,16},{16,32},{32,48},{48,64},{64,80},{80,96},{96,112},{112,128},... | collective-permute-start | bytes 1572872 | tf_op jit(solution)/shard_map/ppermute | solution.py:18
  47.2 19.4 %collective-permute-start = (bf16[1024,384]{1,0:T(8,128)(2,1)}, bf16[1024,384]{1,0:T(8,128)(2,1)}, u32[]{:S(2)}, u32[]{:S(2)}) collective-permute-start(bf16[1024,384]{1,0:T(8,128)(2,1)} %bitcast.122), channel_id=1, source_target_pairs={{0,16},{16,32},{32,48},{48,64},{64,80},{80,96},{96,112},{112,128},... | collective-permute-start | bytes 2359304 | tf_op jit(solution)/shard_map/ppermute | solution.py:18
  54.1 4.2 %copy-start = (f32[2,512,1024]{2,1,0:T(8,128)}, f32[2,512,1024]{2,1,0:T(8,128)S(1)}, u32[]{:S(2)}) copy-start(f32[2,512,1024]{2,1,0:T(8,128)S(1)} %get-tuple-element.22) | copy-start | bytes 12582916
  55.2 3.0 %copy-start.2 = (f32[2,512,1024]{2,1,0:T(8,128)}, f32[2,512,1024]{2,1,0:T(8,128)S(1)}, u32[]{:S(2)}) copy-start(f32[2,512,1024]{2,1,0:T(8,128)S(1)} %get-tuple-element.26) | copy-start | bytes 12582916
  68.9 3.2 %copy-start.3 = (f32[2,512,1024]{2,1,0:T(8,128)}, f32[2,512,1024]{2,1,0:T(8,128)S(1)}, u32[]{:S(2)}) copy-start(f32[2,512,1024]{2,1,0:T(8,128)S(1)} %get-tuple-element.24) | copy-start | bytes 12582916
  69.7 2.3 %copy-start.5 = (f32[2,512,1024]{2,1,0:T(8,128)}, f32[2,512,1024]{2,1,0:T(8,128)S(1)}, u32[]{:S(2)}) copy-start(f32[2,512,1024]{2,1,0:T(8,128)S(1)} %get-tuple-element.28) | copy-start | bytes 12582916
  69.8 39.9 %copy-start.8 = (bf16[1024,2,128]{0,2,1:T(8,128)(2,1)S(1)}, bf16[1024,2,128]{0,2,1:T(8,128)(2,1)}, u32[]{:S(2)}) copy-start(bf16[1024,2,128]{0,2,1:T(8,128)(2,1)} %reshape.106) | copy-start | bytes 1572868
  72.7 60.2 %all-to-all-start.3 = ((f32[64,1,2]{2,1,0:T(1,128)}), f32[64,1,2]{2,1,0:T(1,128)S(1)}, u32[]{:S(2)}, u32[]{:S(2)}) async-start(f32[64,1,2]{2,1,0:T(1,128)} %broadcast_in_dim.71), calls=%async_computation.3 | async-start | bytes 65536 | tf_op jit(solution)/shard_map/all_to_all | solution.py:23
  109.6 3.7 %copy-start.1 = (f32[2,512,1024]{2,1,0:T(8,128)S(1)}, f32[2,512,1024]{2,1,0:T(8,128)}, u32[]{:S(2)}) copy-start(f32[2,512,1024]{2,1,0:T(8,128)} %copy-done) | copy-start | bytes 12582916
  113.3 2.2 %copy-start.6 = (f32[2,512,1024]{2,1,0:T(8,128)S(1)}, f32[2,512,1024]{2,1,0:T(8,128)}, u32[]{:S(2)}) copy-start(f32[2,512,1024]{2,1,0:T(8,128)} %copy-done.5) | copy-start | bytes 12582916
  115.5 2.2 %copy-start.4 = (f32[2,512,1024]{2,1,0:T(8,128)S(1)}, f32[2,512,1024]{2,1,0:T(8,128)}, u32[]{:S(2)}) copy-start(f32[2,512,1024]{2,1,0:T(8,128)} %copy-done.3) | copy-start | bytes 12582916
  117.7 38.8 %copy-start.9 = (bf16[12,768]{1,0:T(8,128)(2,1)S(1)}, bf16[12,768]{1,0:T(8,128)(2,1)}, u32[]{:S(2)}) copy-start(bf16[12,768]{1,0:T(8,128)(2,1)} %param.8) | copy-start | bytes 55300
  117.7 39.4 %copy-start.10 = (bf16[4,512]{1,0:T(4,128)(2,1)S(1)}, bf16[4,512]{1,0:T(4,128)(2,1)}, u32[]{:S(2)}) copy-start(bf16[4,512]{1,0:T(4,128)(2,1)} %param.9) | copy-start | bytes 12292
  133.6 22.4 %all-to-all-start.4 = ((f32[16,1,2]{2,1,0:T(1,128)}), f32[16,1,2]{2,1,0:T(1,128)S(1)}, u32[]{:S(2)}, u32[]{:S(2)}) async-start(f32[16,1,2]{2,1,0:T(1,128)} %broadcast_in_dim.72), calls=%async_computation.4 | async-start | bytes 16384 | tf_op jit(solution)/shard_map/all_to_all | solution.py:23
where the time goes:
time: 158 us
  starting transfers between devices  77 us (49%)
  waiting for transfers between devices  41.2 us (26%)
  local copies, waits for them, and re-layouts  19.3 us (12%)
  matrix products  11.2 us (7%)
  other arithmetic  8.06 us (5%)
    all_to_all x2, starting transfers between devices, from_everyone(): return lax.all_to_all(copies, axis, split_axis=0, concat_axis=0, tiled=True)  53.9 us
    all_to_all x2, waiting for transfers between devices, from_everyone(): return lax.all_to_all(copies, axis, split_axis=0, concat_axis=0, tiled=True)  18.4 us
    all_to_all x1, waiting for transfers between devices, body(): lax.all_to_all(key_rows, 'head', split_axis=1, concat_axis=0, tiled=True)  10.5 us
    ppermute x2, starting transfers between devices, shifted_2(): lax.ppermute(value, axis, [(source, source + steps) for source in range(f...  10 us
    unnamed x25, local copies, waits for them, and re-layouts  7.53 us
    dot_general x4, matrix products, partial_softmax(): jnp.einsum('htu,uhd->thd', rounded, value_cube, preferred_element_type=jn...  7.17 us
    ppermute x2, waiting for transfers between devices, shifted_2(): lax.ppermute(value, axis, [(source, source + steps) for source in range(f...  7.06 us
    all_to_all x1, starting transfers between devices, body(): lax.all_to_all(value_rows, 'head', split_axis=1, concat_axis=0, tiled=True)  5.95 us
  transfers between devices with their start and end apart: 7, of which 5 were waited for; matrix products, arithmetic and copies ran while one was open for 17% of the time, Pallas kernels for 0%

commit v1 on v0

v1 whole, which is shorter than its diff:
```python
import functools
import math

import jax
import jax.numpy as jnp
from jax import lax
from jax.experimental import pallas as pl
from jax.experimental.pallas import tpu as pltpu
from jax.sharding import PartitionSpec as P

DNOPE = 128
DROPE = 64
DV = 128
DQK = 192
HEADS = 2
CLIP = 100.0
SCALE = DQK**-0.5
ROWS = 128
BLK = 1024
TILE = 256
GROUP = 8
MESH = pl.DeviceIdType.MESH
WIDTH = (HEADS * DQK, HEADS * DQK, HEADS * DV)
FAR_ORDER = ((2, 1), (2, 0), (1, 1), (3, 1), (1, 0), (3, 0), (0, 1), (0, 0))


def attention_kernel(
    q_ref,
    k_ref,
    v_ref,
    wq_ref,
    wk_ref,
    out_ref,
    cq_ref,
    ck_ref,
    q_buf,
    k_buf,
    v_buf,
    p_buf,
    acc_buf,
    ones_buf,
    mine_buf,
    near_buf,
    group_buf,
    wide_buf,
    local_sem,
    own_send,
    own_recv,
    far_send,
    far_recv,
    near_send,
    near_recv,
    wide_send,
    wide_recv,
):
    ctx = lax.axis_index("ctx")
    head = lax.axis_index("head")
    core = lax.axis_index("fsdp")
    ctx_count = lax.axis_size("ctx")
    y, x = head // 2, head % 2
    group, member = ctx // GROUP, ctx % GROUP
    groups = ctx_count // GROUP
    owner_core, owner_base = head // 4, 2 * (head % 4)
    target_head = 4 * core + head // 2
    parity = head % 2
    is_own_target = target_head == head

    def peer(dy, dx):
        return lax.rem(y + dy, 4) * 2 + lax.rem(x + dx, 2)

    def place(to_ctx, to_head, to_core):
        return {"ctx": to_ctx, "head": to_head, "fsdp": to_core}

    def near_ctx(step):
        return group * GROUP + lax.rem(member + step, GROUP)

    def wide_ctx(step):
        return lax.rem(group + step, groups) * GROUP + member

    barrier = pltpu.get_barrier_semaphore()

    def greet(where):
        pl.semaphore_signal(barrier, inc=1, device_id=where, device_id_type=MESH)

    for dy, dx in FAR_ORDER[:-1]:
        greet(place(ctx, peer(dy, dx), core))

    @pl.when(ctx > 0)
    def _():
        for dy, dx in FAR_ORDER:
            greet(place(ctx - 1, peer(dy, dx), core))

    for step in range(1, GROUP):
        greet(place(near_ctx(step), head, core))
    for step in range(1, groups):
        for par in range(2):
            greet(place(wide_ctx(step), owner_base + par, owner_core))
    for par in range(2):

        @pl.when(jnp.logical_not((owner_base + par == head) & (owner_core == core)))
        def _():
            greet(place(ctx, owner_base + par, owner_core))

    pl.semaphore_wait(
        barrier,
        7
        + (GROUP - 1)
        + 2 * groups
        + jnp.where(ctx < ctx_count - 1, 8, 0)
        - jnp.where(is_own_target, 1, 0),
    )

    ins = (q_ref, k_ref, v_ref)
    bufs = (q_buf, k_buf, v_buf)

    def columns(ref, t, where):
        return ref.at[:, pl.ds(pl.multiple_of(where * WIDTH[t], 128), WIDTH[t])]

    def landing(t, offset):
        return bufs[t].at[pl.ds(pl.multiple_of(offset + head * ROWS, ROWS), ROWS), :]

    def own_copy(t, n):
        to = peer(*FAR_ORDER[n])
        return pltpu.make_async_remote_copy(
            src_ref=columns(ins[t], t, to),
            dst_ref=landing(t, 0),
            send_sem=own_send.at[t, n],
            recv_sem=own_recv.at[t, n],
            device_id=place(ctx, to, core),
            device_id_type=MESH,
        )

    def far_copy(t, n):
        to = peer(*FAR_ORDER[n])
        return pltpu.make_async_remote_copy(
            src_ref=columns(ins[t], t, to),
            dst_ref=landing(t, BLK),
            send_sem=far_send.at[t - 1, n],
            recv_sem=far_recv.at[t - 1, n],
            device_id=place(ctx + 1, to, core),
            device_id_type=MESH,
        )

    def local_copy(t):
        return pltpu.make_async_copy(columns(ins[t], t, head), landing(t, 0), local_sem.at[t])

    def start_own(t):
        for n in range(7):
            own_copy(t, n).start()
        local_copy(t).start()

    def start_far(t):
        @pl.when(ctx < ctx_count - 1)
        def _():
            for n in range(8):
                far_copy(t, n).start()

    def wait_own(t):
        local_copy(t).wait()
        for n in range(7):
            own_copy(t, n).wait_recv()

    def wait_far(t):
        @pl.when(ctx > 0)
        def _():
            for n in range(8):
                far_copy(t, n).wait_recv()

    start_own(0)
    start_own(1)
    start_far(1)
    start_own(2)
    start_far(2)

    ones_buf[...] = jnp.where(ctx > 0, 1.0, 0.0) * jnp.ones(ones_buf.shape, jnp.bfloat16)

    wait_own(0)
    wait_own(1)
    wait_far(1)

    @pl.when(ctx == 0)
    def _():
        k_buf[BLK:, :] = jnp.broadcast_to(k_buf[0:1, :], (BLK, WIDTH[1]))

    lanes = lax.broadcasted_iota(jnp.int32, (TILE, 2 * 128), 1)
    later = lax.broadcasted_iota(jnp.int32, (TILE, TILE), 0) < lax.broadcasted_iota(
        jnp.int32, (TILE, TILE), 1
    )
    contract = (((1,), (1,)), ((), ()))

    @pl.loop(0, HEADS)
    def _(h):
        window = pl.ds(pl.multiple_of(h * 128, 128), 256)
        valid = (lanes >= DROPE * h) & (lanes < DQK + DROPE * h)
        peak = jnp.full((1, 1), -jnp.inf, jnp.float32)
        for i in range(BLK // TILE):
            rows = slice(i * TILE, (i + 1) * TILE)
            query = jnp.where(valid, q_buf[rows, window], jnp.zeros((), jnp.bfloat16))
            parts = []
            if i > 0:
                parts.append(
                    lax.dot_general(
                        query, k_buf[: i * TILE, window], contract,
                        preferred_element_type=jnp.float32,
                    )
                )
            diagonal = lax.dot_general(
                query, k_buf[rows, window], contract, preferred_element_type=jnp.float32
            )
            parts.append(jnp.where(later, -jnp.inf, diagonal))
            parts.append(
                lax.dot_general(
                    query, k_buf[BLK:, window], contract, preferred_element_type=jnp.float32
                )
            )
            high = functools.reduce(
                jnp.maximum, [jnp.max(part, axis=1, keepdims=True) for part in parts]
            )
            starts = ([0] if i > 0 else []) + [i * TILE, BLK]
            for start, part in zip(starts, parts):
                weights = jnp.exp2((part - high) * (SCALE * math.log2(math.e)))
                p_buf[h, rows, start : start + part.shape[1]] = weights.astype(jnp.bfloat16)
            peak = jnp.maximum(peak, jnp.max(high, axis=0, keepdims=True))
        mine_buf[pl.ds(h, 1), :] = jnp.broadcast_to(peak * SCALE, (1, 128))

    def near_copy(step):
        return pltpu.make_async_remote_copy(
            src_ref=mine_buf,
            dst_ref=near_buf.at[step - 1],
            send_sem=near_send.at[step - 1],
            recv_sem=near_recv.at[step - 1],
            device_id=place(near_ctx(step), head, core),
            device_id_type=MESH,
        )

    for step in range(1, GROUP):
        near_copy(step).start()

    wait_own(2)

    def values(rows, h):
        return v_buf[rows, pl.ds(pl.multiple_of(h * 128, 128), DV)]

    @pl.loop(0, HEADS)
    def _(h):
        for i in range(BLK // TILE):
            rows = slice(i * TILE, (i + 1) * TILE)
            own = slice(0, (i + 1) * TILE)
            right = jnp.concatenate(
                [values(own, h), jnp.ones(((i + 1) * TILE, 128), jnp.bfloat16)], axis=1
            )
            acc_buf[h, rows, :] = jnp.dot(
                p_buf[h, rows, own], right, preferred_element_type=jnp.float32
            )

    for step in range(1, GROUP):
        near_copy(step).wait_recv()
    group_buf[...] = jnp.maximum(mine_buf[...], jnp.max(near_buf[...], axis=0))

    def wide_copy(step, dc):
        return pltpu.make_async_remote_copy(
            src_ref=group_buf,
            dst_ref=wide_buf.at[parity * GROUP + step],
            send_sem=wide_send.at[step, dc],
            recv_sem=wide_recv.at[parity * GROUP + step],
            device_id=place(wide_ctx(step), target_head, lax.rem(core + dc, 2)),
            device_id_type=MESH,
        )

    def wide_arrival(par, step):
        return pltpu.make_async_remote_copy(
            src_ref=group_buf,
            dst_ref=wide_buf.at[par * GROUP + step],
            send_sem=wide_send.at[step, 0],
            recv_sem=wide_recv.at[par * GROUP + step],
            device_id=place(wide_ctx(step), target_head, core),
            device_id_type=MESH,
        )

    for step in range(groups):
        for dc in range(2):
            if step == 0 and dc == 0:

                @pl.when(jnp.logical_not(is_own_target))
                def _():
                    wide_copy(0, 0).start()

                @pl.when(is_own_target)
                def _():
                    wide_buf[pl.ds(parity * GROUP, 1)] = group_buf[...][None]

            else:
                wide_copy(step, dc).start()

    wait_far(2)

    @pl.when(ctx == 0)
    def _():
        v_buf[BLK:, :] = jnp.zeros((BLK, WIDTH[2]), jnp.bfloat16)

    @pl.loop(0, HEADS)
    def _(h):
        right = jnp.concatenate([values(slice(BLK, 2 * BLK), h), ones_buf[...]], axis=1)
        for i in range(BLK // TILE):
            rows = slice(i * TILE, (i + 1) * TILE)
            total = acc_buf[h, rows, :] + jnp.dot(
                p_buf[h, rows, BLK:], right, preferred_element_type=jnp.float32
            )
            out_ref[rows, pl.ds(pl.multiple_of(h * 128, 128), DV)] = (
                total[:, :DV] / total[:, DV:]
            ).astype(jnp.bfloat16)

    for par in range(2):
        for step in range(groups):
            if step == 0:

                @pl.when(
                    jnp.logical_not((owner_base + par == head) & (owner_core == core))
                )
                def _():
                    wide_arrival(par, 0).wait_recv()

            else:
                wide_arrival(par, step).wait_recv()

    half = lax.broadcasted_iota(jnp.int32, (1, 128), 1) < DROPE
    for par in range(2):
        peaks = jnp.max(wide_buf[par * GROUP : (par + 1) * GROUP], axis=0)
        factors = jnp.minimum(1.0, CLIP / peaks)
        roots = jnp.sqrt(factors)
        first, second = factors[0:1], factors[1:2]
        root_first, root_second = roots[0:1], roots[1:2]
        tiles = (
            root_first,
            jnp.where(half, first, root_second),
            jnp.where(half, root_second, second),
        )
        for n, tile in enumerate(tiles):
            at = slice((par * 3 + n) * 128, (par * 3 + n + 1) * 128)
            cq_ref[:, at] = (wq_ref[:, at].astype(jnp.float32) * tile).astype(jnp.bfloat16)
        for n, tile in enumerate((root_first, root_second)):
            at = slice((par * 2 + n) * 128, (par * 2 + n + 1) * 128)
            ck_ref[:, at] = (wk_ref[:, at].astype(jnp.float32) * tile).astype(jnp.bfloat16)

    for t in range(3):
        for n in range(7):
            own_copy(t, n).wait_send()

    @pl.when(ctx < ctx_count - 1)
    def _():
        for t in (1, 2):
            for n in range(8):
                far_copy(t, n).wait_send()

    for step in range(1, GROUP):
        near_copy(step).wait_send()
    for step in range(groups):
        for dc in range(2):
            if step == 0 and dc == 0:

                @pl.when(jnp.logical_not(is_own_target))
                def _():
                    wide_copy(0, 0).wait_send()

            else:
                wide_copy(step, dc).wait_send()


def body(query_rows, key_rows, value_rows, query_weight, key_weight):
    vmem = pl.BlockSpec(memory_space=pltpu.VMEM)
    hbm = pl.BlockSpec(memory_space=pl.ANY)
    groups = lax.axis_size("ctx") // GROUP
    dma = pltpu.SemaphoreType.DMA
    return pl.pallas_call(
        attention_kernel,
        out_shape=(
            jax.ShapeDtypeStruct((BLK, HEADS * DV), jnp.bfloat16),
            jax.ShapeDtypeStruct(query_weight.shape, jnp.bfloat16),
            jax.ShapeDtypeStruct(key_weight.shape, jnp.bfloat16),
        ),
        in_specs=[hbm, hbm, hbm, vmem, vmem],
        out_specs=(vmem, vmem, vmem),
        scratch_shapes=[
            pltpu.VMEM((BLK, WIDTH[0]), jnp.bfloat16),
            pltpu.VMEM((2 * BLK, WIDTH[1]), jnp.bfloat16),
            pltpu.VMEM((2 * BLK, WIDTH[2]), jnp.bfloat16),
            pltpu.VMEM((HEADS, BLK, 2 * BLK), jnp.bfloat16),
            pltpu.VMEM((HEADS, BLK, 2 * DV), jnp.float32),
            pltpu.VMEM((BLK, 128), jnp.bfloat16),
            pltpu.VMEM((HEADS, 128), jnp.float32),
            pltpu.VMEM((GROUP - 1, HEADS, 128), jnp.float32),
            pltpu.VMEM((HEADS, 128), jnp.float32),
            pltpu.VMEM((2 * GROUP, HEADS, 128), jnp.float32),
            dma((3,)),
            dma((3, 7)),
            dma((3, 7)),
            dma((2, 8)),
            dma((2, 8)),
            dma((GROUP - 1,)),
            dma((GROUP - 1,)),
            dma((groups, 2)),
            dma((2 * GROUP,)),
        ],
        compiler_params=pltpu.CompilerParams(
            collective_id=0, has_side_effects=True, vmem_limit_bytes=56 * 1024 * 1024
        ),
        cost_estimate=pl.CostEstimate(
            flops=3_500_000_000, bytes_accessed=3_000_000, transcendentals=3_500_000
        ),
        name="attention",
    )(query_rows, key_rows, value_rows, query_weight, key_weight)


def solution(mesh):
    rows = P(("ctx", "head"), "fsdp")
    weights = P(("ctx", "fsdp"), "head")
    return jax.shard_map(
        body,
        mesh=mesh,
        in_specs=(rows, rows, rows, weights, weights),
        out_specs=(P("ctx", ("fsdp", "head")), weights, weights),
        check_vma=False,
    )
```

time: 158 us -> 94.2 us (0.60)
  the two profiles are of different devices: /device:TPU:1 before, /device:TPU:3 now
where the time goes in v1:
time: 94.2 us; the launch traced here: 93.9 us
  Pallas kernels  90.1 us (96%)
  local copies, waits for them, and re-layouts  3.14 us (3%)
    pallas_call x1, Pallas kernels, body(): pl.pallas_call(attention_kernel, out_shape=(jax.ShapeDtypeStruct((BLK, HE...  90.1 us
    unnamed x7, local copies, waits for them, and re-layouts  3.14 us

profile of v1, /device:TPU:3, one launch (start us, length us, event | category | flops | bytes accessed | tf_op | source)
XLA Modules:
  0.0 93.9 jit_solution(7056036408851161630)
XLA Ops:
  0.6 90.1 %attention.1 = (bf16[1024,256]{1,0:T(8,128)(2,1)}, bf16[12,768]{1,0:T(8,128)(2,1)}, bf16[4,512]{1,0:T(4,128)(2,1)}) custom-call(bf16[128,3072]{1,0:T(8,128)(2,1)} %q_ref.1, bf16[128,3072]{1,0:T(8,128)(2,1)} %k_ref.1, bf16[128,2048]{1,0:T(8,128)(2,1)} %v_ref.1, bf16[12,768]{1,0:T(8,128)(2,1)} %wq_ref.1, bf16[4,512]{1,0:T(4,128)(2,1)} %wk_ref.1), custom_call_target="tpu_custom_call" | custom-call | flops 3500000000 | bytes 3000000 | tf_op jit(solution)/shard_map/attention/pallas_call | solution.py:374
  90.7 0.0 copy-start
  90.7 1.9 %copy.11 = bf16[1024,256]{1,0:T(8,128)(2,1)} copy(bf16[1024,256]{1,0:T(8,128)(2,1)} %get-tuple-element.6) | data formatting | bytes 1048576
  92.6 0.0 copy-done
  92.6 0.0 copy-start.1
  92.6 0.6 copy.12
  93.2 0.1 copy-done.1
  93.3 0.6 copy.13
Async XLA Ops:
  90.7 1.9 %copy-start = (bf16[12,768]{1,0:T(8,128)(2,1)S(1)}, bf16[12,768]{1,0:T(8,128)(2,1)}, u32[]{:S(2)}) copy-start(bf16[12,768]{1,0:T(8,128)(2,1)} %get-tuple-element.7) | copy-start | bytes 55300
  92.6 0.7 copy-start.1

commit v2 on v1

v2 whole, which is shorter than its diff:
```python
import functools
import math

import jax
import jax.numpy as jnp
from jax import lax
from jax.experimental import pallas as pl
from jax.experimental.pallas import tpu as pltpu
from jax.sharding import PartitionSpec as P

DNOPE = 128
DROPE = 64
DV = 128
DQK = 192
HEADS = 2
CLIP = 100.0
SCALE = DQK**-0.5
ROWS = 128
BLK = 1024
TILE = 256
GROUP = 4
HEARD = (1, 2, 4, 8, 16)
MESH = pl.DeviceIdType.MESH
WIDTH = (HEADS * DQK, HEADS * DQK, HEADS * DV)
PEERS = ((2, 1), (2, 0), (1, 1), (3, 1), (1, 0), (3, 0), (0, 1), (0, 0))


def attention_kernel(
    q_ref,
    k_ref,
    v_ref,
    out_ref,
    peak_ref,
    q_buf,
    k_buf,
    v_buf,
    p_buf,
    acc_buf,
    high_buf,
    both_buf,
    far_buf,
    ones_buf,
    mine_buf,
    near_buf,
    part_buf,
    wide_buf,
    local_sem,
    own_send,
    own_recv,
    far_send,
    far_recv,
    near_send,
    near_recv,
    wide_send,
    wide_recv,
    known_sem,
):
    ctx = lax.axis_index("ctx")
    head = lax.axis_index("head")
    core = lax.axis_index("fsdp")
    ctx_count = lax.axis_size("ctx")
    y, x = head // 2, head % 2
    group, member = ctx // GROUP, ctx % GROUP
    groups = ctx_count // GROUP
    owner_core, owner_base = head // 4, 2 * (head % 4)
    target_head = 4 * core + head // 2
    parity = head % 2
    is_own_target = target_head == head

    def peer(dy, dx):
        return lax.rem(y + dy, 4) * 2 + lax.rem(x + dx, 2)

    def place(to_ctx, to_head, to_core):
        return {"ctx": to_ctx, "head": to_head, "fsdp": to_core}

    def ring(step):
        return lax.rem(ctx + step + ctx_count, ctx_count)

    barrier = pltpu.get_barrier_semaphore()

    def greet(where):
        pl.semaphore_signal(barrier, inc=1, device_id=where, device_id_type=MESH)

    for dy, dx in PEERS:
        greet(place(ring(-1), peer(dy, dx), core))
    for dy, dx in PEERS[:-1]:
        greet(place(ctx, peer(dy, dx), core))
    for dy, dx in PEERS:
        greet(place(ctx, peer(dy, dx), 1 - core))
    greet(place(ring(1), head, core))
    pl.semaphore_wait(barrier, 3 * len(PEERS))

    ins = (q_ref, k_ref, v_ref)
    bufs = (q_buf, k_buf, v_buf)

    def columns(ref, t, where):
        return ref.at[:, pl.ds(pl.multiple_of(where * WIDTH[t], 128), WIDTH[t])]

    def landing(t, offset):
        return bufs[t].at[pl.ds(pl.multiple_of(offset + head * ROWS, ROWS), ROWS), :]

    def own_copy(t, n):
        to = peer(*PEERS[n])
        return pltpu.make_async_remote_copy(
            src_ref=columns(ins[t], t, to),
            dst_ref=landing(t, 0),
            send_sem=own_send.at[t, n],
            recv_sem=own_recv.at[t, n],
            device_id=place(ctx, to, core),
            device_id_type=MESH,
        )

    def far_copy(t, n):
        to = peer(*PEERS[n])
        return pltpu.make_async_remote_copy(
            src_ref=columns(ins[t], t, to),
            dst_ref=landing(t, BLK),
            send_sem=far_send.at[t - 1, n],
            recv_sem=far_recv.at[t - 1, n],
            device_id=place(ctx + 1, to, core),
            device_id_type=MESH,
        )

    def local_copy(t):
        return pltpu.make_async_copy(columns(ins[t], t, head), landing(t, 0), local_sem.at[t])

    def start_own(t):
        for n in range(7):
            own_copy(t, n).start()
        local_copy(t).start()

    def start_far(t):
        @pl.when(ctx < ctx_count - 1)
        def _():
            for n in range(8):
                far_copy(t, n).start()

    def wait_own(t):
        local_copy(t).wait()
        for n in range(7):
            own_copy(t, n).wait_recv()

    def wait_far(t):
        @pl.when(ctx > 0)
        def _():
            for n in range(8):
                far_copy(t, n).wait_recv()

    start_own(0)
    start_own(1)
    start_far(1)


    for n, step in enumerate(HEARD):
        for to in (ring(step), ring(-step)):
            pl.semaphore_signal(
                known_sem.at[n], inc=1, device_id=place(to, head, core), device_id_type=MESH
            )
        pl.semaphore_wait(known_sem.at[n], 2)

    ones_buf[...] = jnp.where(ctx > 0, 1.0, 0.0) * jnp.ones(ones_buf.shape, jnp.bfloat16)

    wait_own(0)
    wait_own(1)

    lanes = lax.broadcasted_iota(jnp.int32, (TILE, 2 * 128), 1)
    later = lax.broadcasted_iota(jnp.int32, (TILE, TILE), 0) < lax.broadcasted_iota(
        jnp.int32, (TILE, TILE), 1
    )
    contract = (((1,), (1,)), ((), ()))
    to_log2 = SCALE * math.log2(math.e)

    def head_window(h):
        return pl.ds(pl.multiple_of(h * 128, 128), 256)

    def head_query(h, rows):
        valid = (lanes >= DROPE * h) & (lanes < DQK + DROPE * h)
        return jnp.where(valid, q_buf[rows, head_window(h)], jnp.zeros((), jnp.bfloat16))

    @pl.loop(0, HEADS)
    def _(h):
        window = head_window(h)
        for i in range(BLK // TILE):
            rows = slice(i * TILE, (i + 1) * TILE)
            query = head_query(h, rows)
            diagonal = lax.dot_general(
                query, k_buf[rows, window], contract, preferred_element_type=jnp.float32
            )
            diagonal = jnp.where(later, -jnp.inf, diagonal)
            high = jnp.max(diagonal, axis=1, keepdims=True)
            if i > 0:
                before = lax.dot_general(
                    query, k_buf[: i * TILE, window], contract, preferred_element_type=jnp.float32
                )
                high = jnp.maximum(high, jnp.max(before, axis=1, keepdims=True))
                weights = jnp.exp2((before - high) * to_log2)
                p_buf[h, rows, : i * TILE] = weights.astype(jnp.bfloat16)
            weights = jnp.exp2((diagonal - high) * to_log2)
            p_buf[h, rows, rows] = weights.astype(jnp.bfloat16)
            high_buf[h, rows, :] = jnp.broadcast_to(high, (TILE, 128))

    wait_far(1)

    @pl.when(ctx == 0)
    def _():
        k_buf[BLK:, :] = jnp.broadcast_to(k_buf[0:1, :], (BLK, WIDTH[1]))

    @pl.loop(0, HEADS)
    def _(h):
        peak = jnp.full((1, 1), -jnp.inf, jnp.float32)
        for i in range(BLK // TILE):
            rows = slice(i * TILE, (i + 1) * TILE)
            scores = lax.dot_general(
                head_query(h, rows), k_buf[BLK:, head_window(h)], contract,
                preferred_element_type=jnp.float32,
            )
            far_buf[h, rows, :] = scores
            own_high = high_buf[h, rows, 0:1]
            high = jnp.maximum(own_high, jnp.max(scores, axis=1, keepdims=True))
            both_buf[h, rows, :] = jnp.broadcast_to(high, (TILE, 128))
            peak = jnp.maximum(peak, jnp.max(high, axis=0, keepdims=True))
        mine_buf[pl.ds(h, 1), :] = jnp.broadcast_to(peak * SCALE, (1, 128))

    def near_copy(step, dc):
        return pltpu.make_async_remote_copy(
            src_ref=mine_buf,
            dst_ref=near_buf.at[parity * GROUP + step],
            send_sem=near_send.at[step, dc],
            recv_sem=near_recv.at[parity * GROUP + step],
            device_id=place(
                group * GROUP + lax.rem(member + step, GROUP), target_head, lax.rem(core + dc, 2)
            ),
            device_id_type=MESH,
        )

    def near_arrival(par, step):
        return pltpu.make_async_remote_copy(
            src_ref=mine_buf,
            dst_ref=near_buf.at[par * GROUP + step],
            send_sem=near_send.at[step, 0],
            recv_sem=near_recv.at[par * GROUP + step],
            device_id=place(ctx, target_head, 1 - core),
            device_id_type=MESH,
        )

    for step in reversed(range(GROUP)):
        for dc in range(2):
            if step == 0 and dc == 0:

                @pl.when(jnp.logical_not(is_own_target))
                def _():
                    near_copy(0, 0).start()

                @pl.when(is_own_target)
                def _():
                    near_buf[pl.ds(parity * GROUP, 1)] = mine_buf[...][None]

            else:
                near_copy(step, dc).start()

    @pl.loop(0, HEADS)
    def _(h):
        for i in range(BLK // TILE):
            rows = slice(i * TILE, (i + 1) * TILE)
            own_high = high_buf[h, rows, 0:1]
            high = both_buf[h, rows, 0:1]
            weights = jnp.exp2((far_buf[h, rows, :] - high) * to_log2)
            p_buf[h, rows, BLK:] = weights.astype(jnp.bfloat16)
            high_buf[h, rows, :] = jnp.broadcast_to(
                jnp.exp2((own_high - high) * to_log2), (TILE, 128)
            )

    for par in range(2):

        @pl.when(jnp.logical_not((owner_base + par == head) & (owner_core == core)))
        def _():
            near_arrival(par, 0).wait_recv()

        for step in range(1, GROUP):
            near_arrival(par, step).wait_recv()
        part_buf[par] = jnp.max(near_buf[par * GROUP : (par + 1) * GROUP], axis=0)

    def wide_copy(step):
        return pltpu.make_async_remote_copy(
            src_ref=part_buf,
            dst_ref=wide_buf.at[step - 1],
            send_sem=wide_send.at[step - 1],
            recv_sem=wide_recv.at[step - 1],
            device_id=place(lax.rem(group + step, groups) * GROUP + member, head, core),
            device_id_type=MESH,
        )

    wide_order = sorted(range(1, groups), key=lambda step: -min(step, groups - step))
    for step in wide_order:
        wide_copy(step).start()

    start_own(2)
    start_far(2)

    def values(rows, h):
        return v_buf[rows, pl.ds(pl.multiple_of(h * 128, 128), DV)]

    wait_own(2)

    @pl.loop(0, HEADS)
    def _(h):
        for i in range(BLK // TILE):
            rows = slice(i * TILE, (i + 1) * TILE)
            own = slice(0, (i + 1) * TILE)
            right = jnp.concatenate(
                [values(own, h), jnp.ones(((i + 1) * TILE, 128), jnp.bfloat16)], axis=1
            )
            scale = high_buf[h, rows, :]
            acc_buf[h, rows, :] = jnp.concatenate([scale, scale], axis=1) * jnp.dot(
                p_buf[h, rows, own], right, preferred_element_type=jnp.float32
            )

    wait_far(2)

    @pl.when(ctx == 0)
    def _():
        v_buf[BLK:, :] = jnp.zeros((BLK, WIDTH[2]), jnp.bfloat16)

    @pl.loop(0, HEADS)
    def _(h):
        right = jnp.concatenate([values(slice(BLK, 2 * BLK), h), ones_buf[...]], axis=1)
        for i in range(BLK // TILE):
            rows = slice(i * TILE, (i + 1) * TILE)
            total = acc_buf[h, rows, :] + jnp.dot(
                p_buf[h, rows, BLK:], right, preferred_element_type=jnp.float32
            )
            out_ref[rows, pl.ds(pl.multiple_of(h * 128, 128), DV)] = (
                total[:, :DV] / total[:, DV:]
            ).astype(jnp.bfloat16)

    for step in wide_order:
        wide_copy(step).wait_recv()
    peak_ref[...] = jnp.maximum(part_buf[...], jnp.max(wide_buf[...], axis=0))

    for t in range(3):
        for n in range(7):
            own_copy(t, n).wait_send()

    @pl.when(ctx < ctx_count - 1)
    def _():
        for t in (1, 2):
            for n in range(8):
                far_copy(t, n).wait_send()

    for step in range(GROUP):
        for dc in range(2):
            if step == 0 and dc == 0:

                @pl.when(jnp.logical_not(is_own_target))
                def _():
                    near_copy(0, 0).wait_send()

            else:
                near_copy(step, dc).wait_send()
    for step in wide_order:
        wide_copy(step).wait_send()


def clip_kernel(att_ref, peak_ref, wq_ref, wk_ref, out_ref, cq_ref, ck_ref, hold, in_sem, out_sem):
    def inward(n):
        rows = pl.ds(n * TILE, TILE)
        return pltpu.make_async_copy(att_ref.at[rows, :], hold.at[rows, :], in_sem.at[n])

    def outward(n):
        rows = pl.ds(n * TILE, TILE)
        return pltpu.make_async_copy(hold.at[rows, :], out_ref.at[rows, :], out_sem.at[n])

    for n in range(BLK // TILE):
        inward(n).start()
    for n in range(BLK // TILE):
        inward(n).wait()
        outward(n).start()
    half = lax.broadcasted_iota(jnp.int32, (1, 128), 1) < DROPE
    for par in range(2):
        factors = jnp.minimum(1.0, CLIP / peak_ref[par])
        roots = jnp.sqrt(factors)
        first, second = factors[0:1], factors[1:2]
        root_first, root_second = roots[0:1], roots[1:2]
        tiles = (
            root_first,
            jnp.where(half, first, root_second),
            jnp.where(half, root_second, second),
        )
        for n, tile in enumerate(tiles):
            at = slice((par * 3 + n) * 128, (par * 3 + n + 1) * 128)
            cq_ref[:, at] = (wq_ref[:, at].astype(jnp.float32) * tile).astype(jnp.bfloat16)
        for n, tile in enumerate((root_first, root_second)):
            at = slice((par * 2 + n) * 128, (par * 2 + n + 1) * 128)
            ck_ref[:, at] = (wk_ref[:, at].astype(jnp.float32) * tile).astype(jnp.bfloat16)
    for n in range(BLK // TILE):
        outward(n).wait()


def body(query_rows, key_rows, value_rows, query_weight, key_weight):
    vmem = pl.BlockSpec(memory_space=pltpu.VMEM)
    hbm = pl.BlockSpec(memory_space=pl.ANY)
    groups = lax.axis_size("ctx") // GROUP
    dma = pltpu.SemaphoreType.DMA
    attended, peaks = pl.pallas_call(
        attention_kernel,
        out_shape=(
            jax.ShapeDtypeStruct((BLK, HEADS * DV), jnp.bfloat16),
            jax.ShapeDtypeStruct((2, HEADS, 128), jnp.float32),
        ),
        in_specs=[hbm, hbm, hbm],
        out_specs=(vmem, vmem),
        scratch_shapes=[
            pltpu.VMEM((BLK, WIDTH[0]), jnp.bfloat16),
            pltpu.VMEM((2 * BLK, WIDTH[1]), jnp.bfloat16),
            pltpu.VMEM((2 * BLK, WIDTH[2]), jnp.bfloat16),
            pltpu.VMEM((HEADS, BLK, 2 * BLK), jnp.bfloat16),
            pltpu.VMEM((HEADS, BLK, 2 * DV), jnp.float32),
            pltpu.VMEM((HEADS, BLK, 128), jnp.float32),
            pltpu.VMEM((HEADS, BLK, 128), jnp.float32),
            pltpu.VMEM((HEADS, BLK, BLK), jnp.float32),
            pltpu.VMEM((BLK, 128), jnp.bfloat16),
            pltpu.VMEM((HEADS, 128), jnp.float32),
            pltpu.VMEM((2 * GROUP, HEADS, 128), jnp.float32),
            pltpu.VMEM((2, HEADS, 128), jnp.float32),
            pltpu.VMEM((groups - 1, 2, HEADS, 128), jnp.float32),
            dma((3,)),
            dma((3, 7)),
            dma((3, 7)),
            dma((2, 8)),
            dma((2, 8)),
            dma((GROUP, 2)),
            dma((2 * GROUP,)),
            dma((groups - 1,)),
            dma((groups - 1,)),
            pltpu.SemaphoreType.REGULAR((len(HEARD),)),
        ],
        compiler_params=pltpu.CompilerParams(
            collective_id=0, has_side_effects=True, vmem_limit_bytes=56 * 1024 * 1024
        ),
        cost_estimate=pl.CostEstimate(
            flops=3_500_000_000, bytes_accessed=3_000_000, transcendentals=3_500_000
        ),
        name="attention",
    )(query_rows, key_rows, value_rows)
    return pl.pallas_call(
        clip_kernel,
        out_shape=(
            jax.ShapeDtypeStruct(attended.shape, jnp.bfloat16),
            jax.ShapeDtypeStruct(query_weight.shape, jnp.bfloat16),
            jax.ShapeDtypeStruct(key_weight.shape, jnp.bfloat16),
        ),
        in_specs=[hbm, vmem, vmem, vmem],
        out_specs=(hbm, vmem, vmem),
        scratch_shapes=[
            pltpu.VMEM(attended.shape, jnp.bfloat16),
            dma((BLK // TILE,)),
            dma((BLK // TILE,)),
        ],
        name="clip",
    )(attended, peaks, query_weight, key_weight)


def solution(mesh):
    rows = P(("ctx", "head"), "fsdp")
    weights = P(("ctx", "fsdp"), "head")
    return jax.shard_map(
        body,
        mesh=mesh,
        in_specs=(rows, rows, rows, weights, weights),
        out_specs=(P("ctx", ("fsdp", "head")), weights, weights),
        check_vma=False,
    )
```

time: 94.2 us -> 81.6 us (0.87)
  the two profiles are of different devices: /device:TPU:3 before, /device:TPU:1 now
where the time goes in v2:
time: 81.6 us; the launch traced here: 81.4 us
  Pallas kernels  80.7 us (99%)
    pallas_call x1, Pallas kernels, body(): pl.pallas_call(attention_kernel, out_shape=(jax.ShapeDtypeStruct((BLK, HE...  77.6 us
    pallas_call x1, Pallas kernels, body(): pl.pallas_call(clip_kernel, out_shape=(jax.ShapeDtypeStruct(attended.shap...  3.17 us

profile of v2, /device:TPU:1, one launch (start us, length us, event | category | flops | bytes accessed | tf_op | source)
XLA Modules:
  0.0 81.4 jit_solution(4386063690838860522)
XLA Ops:
  0.6 77.6 %attention.1 = (bf16[1024,256]{1,0:T(8,128)(2,1)}, f32[2,2,128]{2,1,0:T(2,128)}) custom-call(bf16[128,3072]{1,0:T(8,128)(2,1)} %q_ref.1, bf16[128,3072]{1,0:T(8,128)(2,1)} %k_ref.1, bf16[128,2048]{1,0:T(8,128)(2,1)} %v_ref.1), custom_call_target="tpu_custom_call" | custom-call | flops 3500000000 | bytes 3000000 | tf_op jit(solution)/shard_map/attention/pallas_call | solution.py:404
  78.2 3.2 %clip.1 = (bf16[1024,256]{1,0:T(8,128)(2,1)}, bf16[12,768]{1,0:T(8,128)(2,1)}, bf16[4,512]{1,0:T(4,128)(2,1)}) custom-call(bf16[1024,256]{1,0:T(8,128)(2,1)} %get-tuple-element.5.att_ref, f32[2,2,128]{2,1,0:T(2,128)} %get-tuple-element.6.peak_ref, bf16[12,768]{1,0:T(8,128)(2,1)} %wq_ref.1, bf16[4,512]{1,0:T(4,128)(2,1)} %wk_ref.1), custom_call_target="tpu_custom_call" | custom-call | tf_op jit(solution)/shard_map/clip/pallas_call | solution.py:445

commit v3 on v2

--- a/solution.py
+++ b/solution.py
@@ -22,7 +22,7 @@
 HEARD = (1, 2, 4, 8, 16)
 MESH = pl.DeviceIdType.MESH
 WIDTH = (HEADS * DQK, HEADS * DQK, HEADS * DV)
-PEERS = ((2, 1), (2, 0), (1, 1), (3, 1), (1, 0), (3, 0), (0, 1), (0, 0))
+PEERS = ((0, 1), (1, 0), (3, 0), (1, 1), (3, 1), (2, 0), (2, 1), (0, 0))
 
 
 def attention_kernel(
@@ -37,8 +37,7 @@
     p_buf,
     acc_buf,
     high_buf,
-    both_buf,
-    far_buf,
+    s_buf,
     ones_buf,
     mine_buf,
     near_buf,
@@ -96,14 +95,14 @@
     def columns(ref, t, where):
         return ref.at[:, pl.ds(pl.multiple_of(where * WIDTH[t], 128), WIDTH[t])]
 
-    def landing(t, offset):
-        return bufs[t].at[pl.ds(pl.multiple_of(offset + head * ROWS, ROWS), ROWS), :]
+    def landing(t):
+        return bufs[t].at[pl.ds(pl.multiple_of(head * ROWS, ROWS), ROWS), :]
 
     def own_copy(t, n):
         to = peer(*PEERS[n])
         return pltpu.make_async_remote_copy(
             src_ref=columns(ins[t], t, to),
-            dst_ref=landing(t, 0),
+            dst_ref=landing(t),
             send_sem=own_send.at[t, n],
             recv_sem=own_recv.at[t, n],
             device_id=place(ctx, to, core),
@@ -114,7 +113,7 @@
         to = peer(*PEERS[n])
         return pltpu.make_async_remote_copy(
             src_ref=columns(ins[t], t, to),
-            dst_ref=landing(t, BLK),
+            dst_ref=bufs[t].at[pl.ds(BLK + n * ROWS, ROWS), :],
             send_sem=far_send.at[t - 1, n],
             recv_sem=far_recv.at[t - 1, n],
             device_id=place(ctx + 1, to, core),
@@ -122,33 +121,36 @@
         )
 
     def local_copy(t):
-        return pltpu.make_async_copy(columns(ins[t], t, head), landing(t, 0), local_sem.at[t])
-
-    def start_own(t):
+        return pltpu.make_async_copy(columns(ins[t], t, head), landing(t), local_sem.at[t])
+
+    def start(own, far):
         for n in range(7):
-            own_copy(t, n).start()
-        local_copy(t).start()
-
-    def start_far(t):
+            for t in own:
+                own_copy(t, n).start()
+
+            @pl.when(ctx < ctx_count - 1)
+            def _():
+                far_copy(far, n).start()
+
+        for t in own:
+            local_copy(t).start()
+
         @pl.when(ctx < ctx_count - 1)
         def _():
-            for n in range(8):
-                far_copy(t, n).start()
+            far_copy(far, 7).start()
 
     def wait_own(t):
         local_copy(t).wait()
         for n in range(7):
             own_copy(t, n).wait_recv()
 
-    def wait_far(t):
+    def wait_far(t, half):
         @pl.when(ctx > 0)
         def _():
-            for n in range(8):
+            for n in range(4 * half, 4 * half + 4):
                 far_copy(t, n).wait_recv()
 
-    start_own(0)
-    start_own(1)
-    start_far(1)
+    start((0, 1), 1)
 
 
     for n, step in enumerate(HEARD):
@@ -177,49 +179,54 @@
         valid = (lanes >= DROPE * h) & (lanes < DQK + DROPE * h)
         return jnp.where(valid, q_buf[rows, head_window(h)], jnp.zeros((), jnp.bfloat16))
 
+    def lane_max(part):
+        return functools.reduce(
+            jnp.maximum, [part[:, n : n + 128] for n in range(0, part.shape[1], 128)]
+        )
+
+    def head_scores(query, h, keys):
+        return lax.dot_general(
+            query, k_buf[keys, head_window(h)], contract, preferred_element_type=jnp.float32
+        )
+
     @pl.loop(0, HEADS)
     def _(h):
-        window = head_window(h)
         for i in range(BLK // TILE):
             rows = slice(i * TILE, (i + 1) * TILE)
             query = head_query(h, rows)
-            diagonal = lax.dot_general(
-                query, k_buf[rows, window], contract, preferred_element_type=jnp.float32
-            )
-            diagonal = jnp.where(later, -jnp.inf, diagonal)
-            high = jnp.max(diagonal, axis=1, keepdims=True)
+            diagonal = jnp.where(later, -jnp.inf, head_scores(query, h, rows))
+            s_buf[h, rows, rows] = diagonal
+            high = lane_max(diagonal)
             if i > 0:
-                before = lax.dot_general(
-                    query, k_buf[: i * TILE, window], contract, preferred_element_type=jnp.float32
-                )
-                high = jnp.maximum(high, jnp.max(before, axis=1, keepdims=True))
-                weights = jnp.exp2((before - high) * to_log2)
-                p_buf[h, rows, : i * TILE] = weights.astype(jnp.bfloat16)
-            weights = jnp.exp2((diagonal - high) * to_log2)
-            p_buf[h, rows, rows] = weights.astype(jnp.bfloat16)
-            high_buf[h, rows, :] = jnp.broadcast_to(high, (TILE, 128))
-
-    wait_far(1)
-
-    @pl.when(ctx == 0)
-    def _():
-        k_buf[BLK:, :] = jnp.broadcast_to(k_buf[0:1, :], (BLK, WIDTH[1]))
-
-    @pl.loop(0, HEADS)
-    def _(h):
-        peak = jnp.full((1, 1), -jnp.inf, jnp.float32)
-        for i in range(BLK // TILE):
-            rows = slice(i * TILE, (i + 1) * TILE)
-            scores = lax.dot_general(
-                head_query(h, rows), k_buf[BLK:, head_window(h)], contract,
-                preferred_element_type=jnp.float32,
-            )
-            far_buf[h, rows, :] = scores
-            own_high = high_buf[h, rows, 0:1]
-            high = jnp.maximum(own_high, jnp.max(scores, axis=1, keepdims=True))
-            both_buf[h, rows, :] = jnp.broadcast_to(high, (TILE, 128))
-            peak = jnp.maximum(peak, jnp.max(high, axis=0, keepdims=True))
-        mine_buf[pl.ds(h, 1), :] = jnp.broadcast_to(peak * SCALE, (1, 128))
+                before = head_scores(query, h, slice(0, i * TILE))
+                s_buf[h, rows, : i * TILE] = before
+                high = jnp.maximum(high, lane_max(before))
+            high_buf[h, rows, :] = high
+
+    for half in range(2):
+        wait_far(1, half)
+
+        if half == 0:
+
+            @pl.when(ctx == 0)
+            def _():
+                k_buf[BLK:, :] = jnp.broadcast_to(k_buf[0:1, :], (BLK, WIDTH[1]))
+
+        keys = slice(BLK + half * (BLK // 2), BLK + (half + 1) * (BLK // 2))
+
+        @pl.loop(0, HEADS)
+        def _(h):
+            top = jnp.full((TILE, 128), -jnp.inf, jnp.float32)
+            for i in range(BLK // TILE):
+                rows = slice(i * TILE, (i + 1) * TILE)
+                scores = head_scores(head_query(h, rows), h, keys)
+                s_buf[h, rows, keys] = scores
+                high = jnp.maximum(high_buf[h, rows, :], lane_max(scores))
+                high_buf[h, rows, :] = high
+                top = jnp.maximum(top, high)
+            if half == 1:
+                peak = jnp.max(jnp.max(top, axis=0, keepdims=True), axis=1, keepdims=True)
+                mine_buf[pl.ds(h, 1), :] = jnp.broadcast_to(peak * SCALE, (1, 128))
 
     def near_copy(step, dc):
         return pltpu.make_async_remote_copy(
@@ -258,18 +265,6 @@
             else:
                 near_copy(step, dc).start()
 
-    @pl.loop(0, HEADS)
-    def _(h):
-        for i in range(BLK // TILE):
-            rows = slice(i * TILE, (i + 1) * TILE)
-            own_high = high_buf[h, rows, 0:1]
-            high = both_buf[h, rows, 0:1]
-            weights = jnp.exp2((far_buf[h, rows, :] - high) * to_log2)
-            p_buf[h, rows, BLK:] = weights.astype(jnp.bfloat16)
-            high_buf[h, rows, :] = jnp.broadcast_to(
-                jnp.exp2((own_high - high) * to_log2), (TILE, 128)
-            )
-
     for par in range(2):
 
         @pl.when(jnp.logical_not((owner_base + par == head) & (owner_core == core)))
@@ -294,8 +289,16 @@
     for step in wide_order:
         wide_copy(step).start()
 
-    start_own(2)
-    start_far(2)
+    start((2,), 2)
+
+    @pl.loop(0, HEADS)
+    def _(h):
+        for i in range(BLK // TILE):
+            rows = slice(i * TILE, (i + 1) * TILE)
+            high = jnp.max(high_buf[h, rows, :], axis=1, keepdims=True)
+            for keys in (slice(0, (i + 1) * TILE), slice(BLK, 2 * BLK)):
+                weights = jnp.exp2((s_buf[h, rows, keys] - high) * to_log2)
+                p_buf[h, rows, keys] = weights.astype(jnp.bfloat16)
 
     def values(rows, h):
         return v_buf[rows, pl.ds(pl.multiple_of(h * 128, 128), DV)]
@@ -310,12 +313,12 @@
             right = jnp.concatenate(
                 [values(own, h), jnp.ones(((i + 1) * TILE, 128), jnp.bfloat16)], axis=1
             )
-            scale = high_buf[h, rows, :]
-            acc_buf[h, rows, :] = jnp.concatenate([scale, scale], axis=1) * jnp.dot(
+            acc_buf[h, rows, :] = jnp.dot(
                 p_buf[h, rows, own], right, preferred_element_type=jnp.float32
             )
 
-    wait_far(2)
+    wait_far(2, 0)
+    wait_far(2, 1)
 
     @pl.when(ctx == 0)
     def _():
@@ -361,20 +364,8 @@
         wide_copy(step).wait_send()
 
 
-def clip_kernel(att_ref, peak_ref, wq_ref, wk_ref, out_ref, cq_ref, ck_ref, hold, in_sem, out_sem):
-    def inward(n):
-        rows = pl.ds(n * TILE, TILE)
-        return pltpu.make_async_copy(att_ref.at[rows, :], hold.at[rows, :], in_sem.at[n])
-
-    def outward(n):
-        rows = pl.ds(n * TILE, TILE)
-        return pltpu.make_async_copy(hold.at[rows, :], out_ref.at[rows, :], out_sem.at[n])
-
-    for n in range(BLK // TILE):
-        inward(n).start()
-    for n in range(BLK // TILE):
-        inward(n).wait()
-        outward(n).start()
+def clip_kernel(att_ref, peak_ref, wq_ref, wk_ref, out_ref, cq_ref, ck_ref):
+    out_ref[...] = att_ref[...]
     half = lax.broadcasted_iota(jnp.int32, (1, 128), 1) < DROPE
     for par in range(2):
         factors = jnp.minimum(1.0, CLIP / peak_ref[par])
@@ -392,8 +383,6 @@
         for n, tile in enumerate((root_first, root_second)):
             at = slice((par * 2 + n) * 128, (par * 2 + n + 1) * 128)
             ck_ref[:, at] = (wk_ref[:, at].astype(jnp.float32) * tile).astype(jnp.bfloat16)
-    for n in range(BLK // TILE):
-        outward(n).wait()
 
 
 def body(query_rows, key_rows, value_rows, query_weight, key_weight):
@@ -416,8 +405,7 @@
             pltpu.VMEM((HEADS, BLK, 2 * BLK), jnp.bfloat16),
             pltpu.VMEM((HEADS, BLK, 2 * DV), jnp.float32),
             pltpu.VMEM((HEADS, BLK, 128), jnp.float32),
-            pltpu.VMEM((HEADS, BLK, 128), jnp.float32),
-            pltpu.VMEM((HEADS, BLK, BLK), jnp.float32),
+            pltpu.VMEM((HEADS, BLK, 2 * BLK), jnp.float32),
             pltpu.VMEM((BLK, 128), jnp.bfloat16),
             pltpu.VMEM((HEADS, 128), jnp.float32),
             pltpu.VMEM((2 * GROUP, HEADS, 128), jnp.float32),
@@ -449,13 +437,8 @@
             jax.ShapeDtypeStruct(query_weight.shape, jnp.bfloat16),
             jax.ShapeDtypeStruct(key_weight.shape, jnp.bfloat16),
         ),
-        in_specs=[hbm, vmem, vmem, vmem],
-        out_specs=(hbm, vmem, vmem),
-        scratch_shapes=[
-            pltpu.VMEM(attended.shape, jnp.bfloat16),
-            dma((BLK // TILE,)),
-            dma((BLK // TILE,)),
-        ],
+        in_specs=[vmem] * 4,
+        out_specs=(vmem, vmem, vmem),
         name="clip",
     )(attended, peaks, query_weight, key_weight)
 

time: 81.6 us -> 78.1 us (0.957)
  the two profiles are of different devices: /device:TPU:1 before, /device:TPU:32 now
where the time goes in v3:
time: 78.1 us; the launch traced here: 77.9 us
  Pallas kernels  77.3 us (99%)
    pallas_call x1, Pallas kernels, body(): pl.pallas_call(attention_kernel, out_shape=(jax.ShapeDtypeStruct((BLK, HE...  75.4 us
    pallas_call x1, Pallas kernels, body(): pl.pallas_call(clip_kernel, out_shape=(jax.ShapeDtypeStruct(attended.shap...  1.89 us

profile of v3, /device:TPU:32, one launch (start us, length us, event | category | flops | bytes accessed | tf_op | source)
XLA Modules:
  0.0 77.9 jit_solution(3393563990119048137)
XLA Ops:
  0.6 75.4 %attention.1 = (bf16[1024,256]{1,0:T(8,128)(2,1)}, f32[2,2,128]{2,1,0:T(2,128)}) custom-call(bf16[128,3072]{1,0:T(8,128)(2,1)} %q_ref.1, bf16[128,3072]{1,0:T(8,128)(2,1)} %k_ref.1, bf16[128,2048]{1,0:T(8,128)(2,1)} %v_ref.1), custom_call_target="tpu_custom_call" | custom-call | flops 3500000000 | bytes 3000000 | tf_op jit(solution)/shard_map/attention/pallas_call | solution.py:393
  76.0 1.9 %clip.1 = (bf16[1024,256]{1,0:T(8,128)(2,1)}, bf16[12,768]{1,0:T(8,128)(2,1)}, bf16[4,512]{1,0:T(4,128)(2,1)}) custom-call(bf16[1024,256]{1,0:T(8,128)(2,1)} %get-tuple-element.5.att_ref, f32[2,2,128]{2,1,0:T(2,128)} %get-tuple-element.6.peak_ref, bf16[12,768]{1,0:T(8,128)(2,1)} %wq_ref.1, bf16[4,512]{1,0:T(4,128)(2,1)} %wk_ref.1), custom_call_target="tpu_custom_call" | custom-call | tf_op jit(solution)/shard_map/clip/pallas_call | solution.py:433

commit v4 on v3

--- a/solution.py
+++ b/solution.py
@@ -16,6 +16,8 @@
 CLIP = 100.0
 SCALE = DQK**-0.5
 ROWS = 128
+PIECES = 2
+PIECE = ROWS // PIECES
 BLK = 1024
 TILE = 256
 GROUP = 4
@@ -92,30 +94,30 @@
     ins = (q_ref, k_ref, v_ref)
     bufs = (q_buf, k_buf, v_buf)
 
-    def columns(ref, t, where):
-        return ref.at[:, pl.ds(pl.multiple_of(where * WIDTH[t], 128), WIDTH[t])]
-
-    def landing(t):
-        return bufs[t].at[pl.ds(pl.multiple_of(head * ROWS, ROWS), ROWS), :]
-
-    def own_copy(t, n):
+    def columns(ref, t, where, first=0, count=ROWS):
+        return ref.at[pl.ds(first, count), pl.ds(pl.multiple_of(where * WIDTH[t], 128), WIDTH[t])]
+
+    def landing(t, first=0, count=ROWS):
+        return bufs[t].at[pl.ds(pl.multiple_of(head * ROWS + first, PIECE), count), :]
+
+    def own_copy(t, n, piece):
         to = peer(*PEERS[n])
         return pltpu.make_async_remote_copy(
-            src_ref=columns(ins[t], t, to),
-            dst_ref=landing(t),
-            send_sem=own_send.at[t, n],
-            recv_sem=own_recv.at[t, n],
+            src_ref=columns(ins[t], t, to, piece * PIECE, PIECE),
+            dst_ref=landing(t, piece * PIECE, PIECE),
+            send_sem=own_send.at[t, n, piece],
+            recv_sem=own_recv.at[t, n, piece],
             device_id=place(ctx, to, core),
             device_id_type=MESH,
         )
 
-    def far_copy(t, n):
+    def far_copy(t, n, piece):
         to = peer(*PEERS[n])
         return pltpu.make_async_remote_copy(
-            src_ref=columns(ins[t], t, to),
-            dst_ref=bufs[t].at[pl.ds(BLK + n * ROWS, ROWS), :],
-            send_sem=far_send.at[t - 1, n],
-            recv_sem=far_recv.at[t - 1, n],
+            src_ref=columns(ins[t], t, to, piece * PIECE, PIECE),
+            dst_ref=bufs[t].at[pl.ds(BLK + n * ROWS + piece * PIECE, PIECE), :],
+            send_sem=far_send.at[t - 1, n, piece],
+            recv_sem=far_recv.at[t - 1, n, piece],
             device_id=place(ctx + 1, to, core),
             device_id_type=MESH,
         )
@@ -126,29 +128,34 @@
     def start(own, far):
         for n in range(7):
             for t in own:
-                own_copy(t, n).start()
+                for piece in range(PIECES):
+                    own_copy(t, n, piece).start()
 
             @pl.when(ctx < ctx_count - 1)
             def _():
-                far_copy(far, n).start()
+                for piece in range(PIECES):
+                    far_copy(far, n, piece).start()
 
         for t in own:
             local_copy(t).start()
 
         @pl.when(ctx < ctx_count - 1)
         def _():
-            far_copy(far, 7).start()
+            for piece in range(PIECES):
+                far_copy(far, 7, piece).start()
 
     def wait_own(t):
         local_copy(t).wait()
         for n in range(7):
-            own_copy(t, n).wait_recv()
+            for piece in range(PIECES):
+                own_copy(t, n, piece).wait_recv()
 
     def wait_far(t, half):
         @pl.when(ctx > 0)
         def _():
             for n in range(4 * half, 4 * half + 4):
-                far_copy(t, n).wait_recv()
+                for piece in range(PIECES):
+                    far_copy(t, n, piece).wait_recv()
 
     start((0, 1), 1)
 
@@ -342,13 +349,15 @@
 
     for t in range(3):
         for n in range(7):
-            own_copy(t, n).wait_send()
+            for piece in range(PIECES):
+                own_copy(t, n, piece).wait_send()
 
     @pl.when(ctx < ctx_count - 1)
     def _():
         for t in (1, 2):
             for n in range(8):
-                far_copy(t, n).wait_send()
+                for piece in range(PIECES):
+                    far_copy(t, n, piece).wait_send()
 
     for step in range(GROUP):
         for dc in range(2):
@@ -412,10 +421,10 @@
             pltpu.VMEM((2, HEADS, 128), jnp.float32),
             pltpu.VMEM((groups - 1, 2, HEADS, 128), jnp.float32),
             dma((3,)),
-            dma((3, 7)),
-            dma((3, 7)),
-            dma((2, 8)),
-            dma((2, 8)),
+            dma((3, 7, PIECES)),
+            dma((3, 7, PIECES)),
+            dma((2, 8, PIECES)),
+            dma((2, 8, PIECES)),
             dma((GROUP, 2)),
             dma((2 * GROUP,)),
             dma((groups - 1,)),

time: 78.1 us -> 78.8 us (level)
  no operation moved by 1% of the time
where the time goes in v4:
time: 78.8 us; the launch traced here: 78.6 us
  Pallas kernels  78 us (99%)
    pallas_call x1, Pallas kernels, body(): pl.pallas_call(attention_kernel, out_shape=(jax.ShapeDtypeStruct((BLK, HE...  76.1 us
    pallas_call x1, Pallas kernels, body(): pl.pallas_call(clip_kernel, out_shape=(jax.ShapeDtypeStruct(attended.shap...  1.89 us

profile of v4, /device:TPU:32, one launch (start us, length us, event | category | flops | bytes accessed | tf_op | source)
XLA Modules:
  0.0 78.6 jit_solution(12736355274428093866)
XLA Ops:
  0.6 76.1 %attention.1 = (bf16[1024,256]{1,0:T(8,128)(2,1)}, f32[2,2,128]{2,1,0:T(2,128)}) custom-call(bf16[128,3072]{1,0:T(8,128)(2,1)} %q_ref.1, bf16[128,3072]{1,0:T(8,128)(2,1)} %k_ref.1, bf16[128,2048]{1,0:T(8,128)(2,1)} %v_ref.1), custom_call_target="tpu_custom_call" | custom-call | flops 3500000000 | bytes 3000000 | tf_op jit(solution)/shard_map/attention/pallas_call | solution.py:402
  76.7 1.9 %clip.1 = (bf16[1024,256]{1,0:T(8,128)(2,1)}, bf16[12,768]{1,0:T(8,128)(2,1)}, bf16[4,512]{1,0:T(4,128)(2,1)}) custom-call(bf16[1024,256]{1,0:T(8,128)(2,1)} %get-tuple-element.5.att_ref, f32[2,2,128]{2,1,0:T(2,128)} %get-tuple-element.6.peak_ref, bf16[12,768]{1,0:T(8,128)(2,1)} %wq_ref.1, bf16[4,512]{1,0:T(4,128)(2,1)} %wk_ref.1), custom_call_target="tpu_custom_call" | custom-call | tf_op jit(solution)/shard_map/clip/pallas_call | solution.py:442
